TPU v7x, 256 devices: a whole 4x4x8 slice. The times are simulated.
256 devices in a mesh: replica: 16 (over y_lo, z), fsdp: 16 (over y_hi, x, core).
Axes of the slice: x: 4, y: 4 (y_hi: 2, y_lo: 2; y = y_hi * 2 + y_lo), z: 8, core: 2. Of those that a mesh axis runs over, the one named last changes fastest.
Arguments:
- inputs: bfloat16 [98304, 4096], P(('replica', 'fsdp')), may hold values from -24 to 24
- projection: bfloat16 [16, 4096, 1024], P('replica', 'fsdp'), may hold values from -0.09375 to 0.09375
- cotangent: bfloat16 [98304, 1024], P(('replica', 'fsdp')), may hold values from -0.07470703 to 0.07470703
- pseudo_grad: bfloat16 [16, 2048, 4096], P('replica', 'fsdp'), may hold values from -6 to 6
- outer_params: float32 [2048, 4096], P('fsdp', 'replica'), may hold values from -0.125 to 0.125
- outer_momentum: float32 [2048, 4096], P('fsdp', 'replica'), may hold values from -1.5 to 1.5
Outputs:
- keys_values: bfloat16 [98304, 1024], P(('replica', 'fsdp'))
- proj_grad: float32 [16, 4096, 1024], P('replica', 'fsdp')
- new_params: float32 [2048, 4096], P('fsdp', 'replica')
- new_momentum: float32 [2048, 4096], P('fsdp', 'replica')
- local_weights: bfloat16 [2048, 4096], P('fsdp')
All inputs are finite; a program needn't handle non-finite values.
Results may differ from a plain program's by a relative error of at most 0.0029.
Values may be sent and summed in bfloat16 or wider, within the bound.
A program may use at most 128 MiB of HBM per device.

v0:
```python
import jax
import jax.numpy as jnp
from jax import lax
from jax.sharding import PartitionSpec as P

outer_rate = 0.7
outer_beta = 0.9


def on_device(inputs, projection, cotangent, pseudo_grad, outer_params, outer_momentum):
    weight_shard = projection[0]
    columns = inputs
    keys_values = jnp.dot(
        columns,
        lax.all_gather(weight_shard, "fsdp", axis=0, tiled=True),
        preferred_element_type=jnp.float32,
    ).astype(jnp.bfloat16)
    columns = inputs
    partial_term = jnp.einsum("td,tc->dc", columns, cotangent, preferred_element_type=jnp.float32)
    gradient = lax.psum_scatter(
        lax.optimization_barrier(partial_term.astype(jnp.bfloat16)).astype(jnp.float32),
        "fsdp",
        scatter_dimension=0,
        tiled=True,
    )
    proj_grad = gradient[None]
    replicas = lax.axis_size("replica")
    local_delta = pseudo_grad[0].astype(jnp.float32)
    summed = lax.psum(local_delta, "replica")
    full_params, full_moment = (
        lax.all_gather(outer_params, "replica", axis=1, tiled=True),
        lax.all_gather(outer_momentum, "replica", axis=1, tiled=True),
    )
    average = summed / replicas
    moment = outer_beta * full_moment + average
    params = full_params - outer_rate * (outer_beta * moment + average)
    local_weights = params.astype(jnp.bfloat16)
    share_cols = outer_params.shape[1]
    offset = lax.axis_index("replica") * share_cols
    new_params = lax.dynamic_slice_in_dim(params, offset, share_cols, 1)
    new_momentum = lax.dynamic_slice_in_dim(moment, offset, share_cols, 1)
    return (keys_values, proj_grad, new_params, new_momentum, local_weights)


def solution(mesh):
    return jax.shard_map(
        on_device,
        mesh=mesh,
        in_specs=(
            P(("replica", "fsdp"), None),
            P("replica", "fsdp", None),
            P(("replica", "fsdp"), None),
            P("replica", "fsdp", None),
            P("fsdp", "replica"),
            P("fsdp", "replica"),
        ),
        out_specs=(
            P(("replica", "fsdp"), None),
            P("replica", "fsdp", None),
            P("fsdp", "replica"),
            P("fsdp", "replica"),
            P("fsdp", None),
        ),
        check_vma=False,
    )
```

profile of v0, /device:TPU:24, one launch (start us, length us, event | category | flops | bytes accessed | tf_op | source)
XLA Modules:
  0.0 537.2 jit_solution(9725726964979526608)
XLA Ops:
  7.2 0.0 copy-start
  7.2 0.0 all-reduce.2.cloned.1.call-start
  7.2 2.9 bitcast_convert_fusion
  10.1 0.0 all-reduce.2.cloned.1.call-update
  10.2 0.0 all-gather.5.cloned.1.call-start
  10.2 0.7 all-gather.5.cloned.1.call-update
  10.9 0.0 all-gather.7.cloned.1.call-start
  11.0 0.7 all-gather.7.cloned.1.call-update
  11.7 0.0 all-gather.9.cloned.1.call-start
  11.7 0.5 all-gather.9.cloned.1.call-update
  12.2 0.0 reduce-scatter.2.cloned.1.call-start
  12.3 0.0 copy-done
  12.3 7.9 %convolution_convert_fusion = bf16[4096,1024]{1,0:T(8,128)(2,1)} fusion(bf16[384,4096]{1,0:T(8,128)(2,1)S(1)} %copy-done, bf16[384,1024]{1,0:T(8,128)(2,1)} %param.8), kind=kOutput, calls=%fused_computation.2 | convolution fusion | flops 3225419776 | bytes 12320768 | tf_op jit(solution)/shard_map/td,tc->dc/dot_general | solution.py:19
  20.1 11.3 %convert_element_type.20 = f32[4096,1024]{1,0:T(8,128)} convert(bf16[4096,1024]{1,0:T(8,128)(2,1)} %convolution_convert_fusion) | non-fusion elementwise | flops 4194304 | bytes 25165824 | tf_op jit(solution)/shard_map/convert_element_type | solution.py:21
  31.4 0.0 reduce-scatter.2.cloned.1.call-update
  31.4 123.3 %all-reduce.2.cloned.1.call-done = f32[128,4096]{1,0:T(8,128)} async-done(((f32[128,4096]{1,0:T(8,128)}), f32[128,4096]{1,0:T(8,128)}) %all-reduce.2.cloned.1.call-update) | async-done | bytes 2097168 | tf_op jit(solution)/shard_map/psum | solution.py:29
  154.7 70.7 %all-gather.5.cloned.1.call-done = f32[128,4096]{1,0:T(8,128)} async-done(((f32[128,256]{1,0:T(8,128)}), f32[128,4096]{1,0:T(8,128)}) %all-gather.5.cloned.1.call-update) | async-done | bytes 2097168 | tf_op jit(solution)/shard_map/all_gather | solution.py:31
  225.4 70.6 %all-gather.7.cloned.1.call-done = f32[128,4096]{1,0:T(8,128)} async-done(((f32[128,256]{1,0:T(8,128)}), f32[128,4096]{1,0:T(8,128)}) %all-gather.7.cloned.1.call-update) | async-done | bytes 2097168 | tf_op jit(solution)/shard_map/all_gather | solution.py:32
  296.1 4.5 fusion.5
  300.5 0.7 constant_dynamic-slice_fusion
  301.3 71.6 %all-gather.9.cloned.1.call-done = bf16[1,4096,1024]{2,1,0:T(8,128)(2,1)} async-done(((bf16[1,256,1024]{2,1,0:T(8,128)(2,1)}), bf16[1,4096,1024]{2,1,0:T(8,128)(2,1)}) %all-gather.9.cloned.1.call-update) | async-done | bytes 8388624 | tf_op jit(solution)/shard_map/all_gather | solution.py:15
  372.9 6.8 %fusion.2 = bf16[384,1024]{1,0:T(8,128)(2,1)} fusion(bf16[384,4096]{1,0:T(8,128)(2,1)S(1)} %copy-done, bf16[1,4096,1024]{2,1,0:T(8,128)(2,1)} %all-gather.9.cloned.1.call-done), kind=kOutput, calls=%fused_computation.5 | convolution fusion | flops 3221618688 | bytes 12320768 | tf_op jit(solution)/shard_map/dot_general | solution.py:13
  379.6 151.1 %reduce-scatter.2.cloned.1.call-done = f32[256,1024]{1,0:T(8,128)} async-done(((f32[4096,1024]{1,0:T(8,128)}), f32[256,1024]{1,0:T(8,128)}) %reduce-scatter.2.cloned.1.call-update) | async-done | bytes 1048592 | tf_op jit(solution)/shard_map/reduce_scatter | solution.py:20
Async XLA Ops:
  7.2 5.1 copy-start
  7.2 147.6 %all-reduce.2.cloned.1.call-start = ((), (), s32[]{:S(2)}) async-start(), calls=%async_computation.4 | async-start | bytes 4194304 | tf_op jit(solution)/shard_map/psum | solution.py:29
  10.2 215.3 %all-gather.5.cloned.1.call-start = ((), (), s32[]{:S(2)}) async-start(), calls=%async_computation.2 | async-start | bytes 2228224 | tf_op jit(solution)/shard_map/all_gather | solution.py:31
  10.9 285.1 %all-gather.7.cloned.1.call-start = ((), (), s32[]{:S(2)}) async-start(), calls=%async_computation.3 | async-start | bytes 2228224 | tf_op jit(solution)/shard_map/all_gather | solution.py:32
  11.7 361.2 %all-gather.9.cloned.1.call-start = ((), (), s32[]{:S(2)}) async-start(), calls=%async_computation.5 | async-start | bytes 8912896 | tf_op jit(solution)/shard_map/all_gather | solution.py:15
  12.2 518.5 %reduce-scatter.2.cloned.1.call-start = ((), (), s32[]{:S(2)}) async-start(), calls=%async_computation.1 | async-start | bytes 17825792 | tf_op jit(solution)/shard_map/reduce_scatter | solution.py:20
Sparse Core Ops, SparseCore 0:
  10.7 144.0 all-reduce.1
  156.5 68.8 all-gather.4
  227.2 68.7 all-gather.6
  298.6 74.1 all-gather.8
  378.0 152.6 reduce-scatter.1
where the time goes:
time: 540 us; the launch traced here: 537 us
  waiting for transfers between devices  489 us (91%)
  other arithmetic  18.7 us (3%)
  matrix products  14.6 us (3%)
  between operations  13.8 us (3%)
    reduce_scatter x1, waiting for transfers between devices, on_device(): lax.psum_scatter(lax.optimization_barrier(partial_term.astype(jnp.bfloat1...  151 us
    psum x1, waiting for transfers between devices, on_device(): summed = lax.psum(local_delta, 'replica')  123 us
    all_gather x1, waiting for transfers between devices, on_device(): lax.all_gather(weight_shard, 'fsdp', axis=0, tiled=True)  71.6 us
    all_gather x1, waiting for transfers between devices, on_device(): lax.all_gather(outer_params, 'replica', axis=1, tiled=True)  70.7 us
    all_gather x1, waiting for transfers between devices, on_device(): lax.all_gather(outer_momentum, 'replica', axis=1, tiled=True)  70.6 us
    convert_element_type x1, other arithmetic, on_device(): lax.optimization_barrier(partial_term.astype(jnp.bfloat16))  11.3 us
  transfers between devices with their start and end apart: 5, of which 5 were waited for; matrix products, arithmetic and copies ran while one was open for 6% of the time, Pallas kernels for 0%

commit v1 on v0

v1 whole, which is shorter than its diff:
```python
import jax
import jax.numpy as jnp
from jax import lax
from jax.experimental import pallas as pl
from jax.experimental.pallas import tpu as pltpu
from jax.sharding import PartitionSpec as P

outer_rate = 0.7
outer_beta = 0.9

MESH = pl.DeviceIdType.MESH
bf16 = jnp.bfloat16
f32 = jnp.float32

TOK = 384
D = 4096
HALF = 2048
KV = 1024
ROWS = 256
CUT = 160
MID1 = CUT // 2
MID2 = CUT + (ROWS - CUT) // 2
FR = 128
FC = 256

MESSAGES = (
    ["yP1", "yP2_0", "yP2_1", "yP2_3", "yP2_2a", "yP2_2b"]
    + [d + k for d in ("xp", "xm") for k in ("P2", "P1", "Q1", "fP2", "fP1", "fQ1")]
    + ["xs%d" % r for r in range(8)]
    + ["cs", "kv0", "kv1"]
    + ["b%s%d" % (d, y) for d in "pm" for y in (0, 1)]
    + ["c%s%d%s" % (d, y, h) for d in "pm" for y in (0, 1) for h in "ab"]
    + ["d%d" % x for x in range(4)]
    + ["e", "gp", "gm", "hp", "hm"]
    + ["z%s%d" % (d, k) for d in "pm" for k in (4, 3, 2, 1)]
    + ["yo", "yl"]
    + ["g%s%d" % (d, k) for d in "pm" for k in (1, 2, 3, 4)]
)
NUMBER = {name: i for i, name in enumerate(MESSAGES)}


def rel(dx, dy):
    return (dx % 4) + 4 * dy


def kernel(
    x_hbm, w_hbm, c_hbm, ps_hbm, op_hbm, om_hbm,
    kv_out, grad_out, np_out, nm_out, lw_out,
    Xb, Cb, Wb, TO, T, SB, KVs, KVo, KVr, KVb,
    rap, ram, rd, rbp, rbm, re, rgp, rgm, rhp, rhm, G,
    PSb, zq4p, zq4m, zs, zq, ZS, yr, OPb, OMb, NP, NM, LW,
    ssem, rsem, lsem,
):
    r_id = lax.axis_index("replica")
    f_id = lax.axis_index("fsdp")
    z = lax.rem(r_id, 8)
    ylo = r_id // 8
    c = lax.rem(f_id, 2)
    x = lax.rem(f_id // 2, 4)
    yh = f_id // 8

    def device(x, yh, z, ylo, c):
        return (ylo * 8 + z, yh * 8 + x * 2 + c)

    XP = device(lax.rem(x + 1, 4), yh, z, ylo, c)
    XM = device(lax.rem(x + 3, 4), yh, z, ylo, c)
    Y = device(x, 1 - yh, z, ylo, c)
    YL = device(x, yh, z, 1 - ylo, c)
    ZP = device(x, yh, lax.rem(z + 1, 8), ylo, c)
    ZM = device(x, yh, lax.rem(z + 7, 8), ylo, c)
    SIB = device(x, yh, z, ylo, 1 - c)

    barrier = pltpu.get_barrier_semaphore()
    for dev in (XP, XM, Y, YL, ZP, ZM, SIB):
        pl.semaphore_signal(barrier, inc=1, device_id=dev, device_id_type=MESH)

    def columns(r, core):
        chip = (yh if r < 4 else 1 - yh) * 4 + lax.rem(x + r % 4, 4)
        return pl.ds(pl.multiple_of(chip * 512 + core * 256, 256), 256)

    def lanes(r):
        return pl.ds(r * 256, 256)

    locals_ = []

    def load(src, dst):
        cp = pltpu.make_async_copy(src, dst, lsem.at[len(locals_)])
        cp.start()
        locals_.append(cp)
        return cp

    load_x = [load(x_hbm.at[:, columns(r, c)], Xb.at[0, :, lanes(r)]) for r in range(8)]
    load_c = load(c_hbm, Cb.at[0])
    load_w = load(w_hbm.at[0], Wb.at[0])
    load_ps = []
    for dz in (4, 3, 5, 2, 6, 1, 7, 0):
        for b in range(2):
            cols = pl.ds(pl.multiple_of(b * HALF + lax.rem(z + dz, 8) * FC, FC), FC)
            load_ps.append(load(ps_hbm.at[0, :, cols], PSb.at[dz, b]))
    load_o = [load(op_hbm, OPb), load(om_hbm, OMb)]

    sent = {}

    def send(name, src, dst, dev):
        i = NUMBER[name]
        cp = pltpu.make_async_remote_copy(
            src_ref=src, dst_ref=dst, send_sem=ssem.at[i], recv_sem=rsem.at[i],
            device_id=dev, device_id_type=MESH,
        )
        cp.start()
        sent[name] = cp

    def arrived(*names):
        for name in names:
            sent[name].wait_recv()

    def rows_loop(n, body):
        @pl.loop(0, n // 16)
        def _(i):
            body(lambda base: pl.ds(pl.multiple_of(base + i * 16, 16), 16))

    contract = (((0,), (0,)), ((), ()))

    def own_term(r):
        @pl.loop(0, 2)
        def _(j):
            cols = pl.ds(pl.multiple_of(j * 512, 512), 512)
            TO[r, :, cols] = lax.dot_general(
                Xb[0, :, lanes(r)], Cb[0, :, cols], contract, preferred_element_type=f32
            ).astype(bf16)

    def both_terms(r):
        @pl.loop(0, 2)
        def _(j):
            cols = pl.ds(pl.multiple_of(j * 512, 512), 512)
            other = lax.dot_general(
                Xb[1, :, lanes(r)], Cb[1, :, cols], contract, preferred_element_type=f32
            ).astype(bf16)
            total = TO[r, :, cols].astype(f32) + other.astype(f32)
            T[r, :, cols] = total
            SB[r, :, cols] = total.astype(bf16)

    load_c.wait()
    for cp in load_x:
        cp.wait()
    own_term(rel(2, 0))
    own_term(rel(2, 1))

    pl.semaphore_wait(barrier, 7)

    send("xpP2", w_hbm.at[0, CUT:ROWS], Wb.at[rel(3, 0), CUT:ROWS], XP)
    send("xmP2", w_hbm.at[0, CUT:ROWS], Wb.at[rel(1, 0), CUT:ROWS], XM)
    send("yP1", w_hbm.at[0, 0:CUT], Wb.at[rel(0, 1), 0:CUT], Y)
    send("cs", c_hbm, Cb.at[1], SIB)
    for r in (rel(2, 0), rel(2, 1), rel(1, 1), rel(3, 1), rel(1, 0), rel(3, 0), rel(0, 1), rel(0, 0)):
        send("xs%d" % r, x_hbm.at[:, columns(r, 1 - c)], Xb.at[1, :, lanes(r)], SIB)
    for cp in load_ps:
        cp.wait()
    send("zp4", PSb.at[4, 0], zq4p, ZP)
    send("zm4", PSb.at[4, 1], zq4m, ZM)
    send("xpP1", w_hbm.at[0, 0:CUT], Wb.at[rel(3, 0), 0:CUT], XP)
    send("xmP1", w_hbm.at[0, 0:CUT], Wb.at[rel(1, 0), 0:CUT], XM)
    send("yP2_0", w_hbm.at[0, CUT:ROWS], Wb.at[rel(0, 1), CUT:ROWS], Y)

    def z3():
        arrived("zp4", "zm4")

        def body(at):
            s = at(0)
            zs[0, 0, 0, s] = PSb[3, 0, s].astype(f32) + zq4p[s].astype(f32)
            zs[0, 0, 1, s] = PSb[3, 1, s].astype(f32)
            zs[1, 0, 0, s] = PSb[5, 0, s].astype(f32)
            zs[1, 0, 1, s] = PSb[5, 1, s].astype(f32) + zq4m[s].astype(f32)

        rows_loop(FR, body)
        send("zp3", zs.at[0, 0], zq.at[0, 0], ZP)
        send("zm3", zs.at[1, 0], zq.at[1, 0], ZM)

    def z2():
        arrived("zp3", "zm3")

        def body(at):
            s = at(0)
            for b in range(2):
                zs[0, 1, b, s] = PSb[2, b, s].astype(f32) + zq[0, 0, b, s]
                zs[1, 1, b, s] = PSb[6, b, s].astype(f32) + zq[1, 0, b, s]

        rows_loop(FR, body)
        send("zp2", zs.at[0, 1], zq.at[0, 1], ZP)
        send("zm2", zs.at[1, 1], zq.at[1, 1], ZM)

    def z1():
        arrived("zp2", "zm2")

        def body(at):
            s = at(0)
            for b in range(2):
                zs[0, 2, b, s] = PSb[1, b, s].astype(f32) + zq[0, 1, b, s]
                zs[1, 2, b, s] = PSb[7, b, s].astype(f32) + zq[1, 1, b, s]

        rows_loop(FR, body)
        send("zp1", zs.at[0, 2], zq.at[0, 2], ZP)
        send("zm1", zs.at[1, 2], zq.at[1, 2], ZM)

    def z0():
        arrived("zp1", "zm1")

        def body(at):
            s = at(0)
            for b in range(2):
                ZS[b, s] = PSb[0, b, s].astype(f32) + zq[0, 2, b, s] + zq[1, 2, b, s]

        rows_loop(FR, body)
        send("yo", ZS.at[1 - ylo], yr, YL)

    stores = []

    def store(src, dst):
        cp = pltpu.make_async_copy(src, dst, lsem.at[len(locals_) + len(stores)])
        cp.start()
        stores.append(cp)

    def store_lw(dz, blocks=(0, 1)):
        for b in blocks:
            cols = pl.ds(pl.multiple_of(b * HALF + lax.rem(z + dz, 8) * FC, FC), FC)
            store(LW.at[dz, b], lw_out.at[:, cols])

    def outer_step():
        for cp in load_o:
            cp.wait()
        arrived("yo")

        def body(at):
            s = at(0)
            average = (ZS[ylo, s] + yr[s]) * (1.0 / 16)
            moment = outer_beta * OMb[s] + average
            params = OPb[s] - outer_rate * (outer_beta * moment + average)
            NM[s] = moment
            NP[s] = params
            LW[0, ylo, s] = params.astype(bf16)

        rows_loop(FR, body)
        send("yl", LW.at[0, ylo], LW.at[0, ylo], YL)
        store(NM, nm_out)
        store(NP, np_out)

    def g1():
        arrived("yl")
        send("gp1", LW.at[0], LW.at[7], ZP)
        send("gm1", LW.at[0], LW.at[1], ZM)
        store_lw(0)

    def g2():
        arrived("gp1", "gm1")
        send("gp2", LW.at[7], LW.at[6], ZP)
        send("gm2", LW.at[1], LW.at[2], ZM)
        store_lw(7)
        store_lw(1)

    def g3():
        arrived("gp2", "gm2")
        send("gp3", LW.at[6], LW.at[5], ZP)
        send("gm3", LW.at[2], LW.at[3], ZM)
        store_lw(6)
        store_lw(2)

    def g4():
        arrived("gp3", "gm3")
        send("gp4", LW.at[5, 0], LW.at[4, 0], ZP)
        send("gm4", LW.at[3, 1], LW.at[4, 1], ZM)
        store_lw(5)
        store_lw(3)

    def g5():
        arrived("gp4", "gm4")
        store_lw(4)

    def a_p2():
        arrived("xpP2", "xmP2")
        send("xpfP2", Wb.at[rel(3, 0), CUT:MID2], Wb.at[rel(2, 0), CUT:MID2], XP)
        send("xmfP2", Wb.at[rel(1, 0), MID2:ROWS], Wb.at[rel(2, 0), MID2:ROWS], XM)
        send("yP2_3", Wb.at[rel(3, 0), CUT:ROWS], Wb.at[rel(3, 1), CUT:ROWS], Y)
        send("yP2_1", Wb.at[rel(1, 0), CUT:ROWS], Wb.at[rel(1, 1), CUT:ROWS], Y)

    def a_q1():
        arrived("yP1")
        send("xpQ1", Wb.at[rel(0, 1), 0:CUT], Wb.at[rel(3, 1), 0:CUT], XP)
        send("xmQ1", Wb.at[rel(0, 1), 0:CUT], Wb.at[rel(1, 1), 0:CUT], XM)

    def a_p1():
        arrived("xpP1", "xmP1")
        send("xpfP1", Wb.at[rel(3, 0), 0:MID1], Wb.at[rel(2, 0), 0:MID1], XP)
        send("xmfP1", Wb.at[rel(1, 0), MID1:CUT], Wb.at[rel(2, 0), MID1:CUT], XM)

    def a_p2far():
        arrived("xpfP2", "xmfP2")
        send("yP2_2a", Wb.at[rel(2, 0), CUT:MID2], Wb.at[rel(2, 1), CUT:MID2], Y)
        send("yP2_2b", Wb.at[rel(2, 0), MID2:ROWS], Wb.at[rel(2, 1), MID2:ROWS], Y)

    def a_fq1():
        arrived("xpQ1", "xmQ1")
        send("xpfQ1", Wb.at[rel(3, 1), 0:MID1], Wb.at[rel(2, 1), 0:MID1], XP)
        send("xmfQ1", Wb.at[rel(1, 1), MID1:CUT], Wb.at[rel(2, 1), MID1:CUT], XM)

    def b_send(dy):
        r = rel(2, dy)
        send("bp%d" % dy, SB.at[r, 0:MID1], rap.at[dy], XP)
        send("bm%d" % dy, SB.at[r, MID1:CUT], ram.at[dy], XM)

    def d_send(dx):
        send("d%d" % dx, SB.at[rel(dx, 1), CUT:ROWS], rd.at[dx], Y)

    def c_plain(dx, dy):
        if dx == 1:
            send("cp%db" % dy, SB.at[rel(1, dy), MID1:CUT], rbp.at[dy, MID1:CUT], XP)
        else:
            send("cm%db" % dy, SB.at[rel(3, dy), 0:MID1], rbm.at[dy, 0:MID1], XM)

    def c_added(dy):
        arrived("bp%d" % dy, "bm%d" % dy)

        def body(at):
            s, t = at(0), at(MID1)
            SB[rel(1, dy), s] = (T[rel(1, dy), s] + rap[dy, s].astype(f32)).astype(bf16)
            SB[rel(3, dy), t] = (T[rel(3, dy), t] + ram[dy, s].astype(f32)).astype(bf16)

        rows_loop(MID1, body)
        send("cp%da" % dy, SB.at[rel(1, dy), 0:MID1], rbp.at[dy, 0:MID1], XP)
        send("cm%da" % dy, SB.at[rel(3, dy), MID1:CUT], rbm.at[dy, MID1:CUT], XM)

    def e_send():
        arrived("cp1a", "cp1b", "cm1a", "cm1b")

        def body(at):
            s = at(0)
            total = T[rel(0, 1), s] + rbp[1, s].astype(f32) + rbm[1, s].astype(f32)
            SB[rel(0, 1), s] = total.astype(bf16)

        rows_loop(CUT, body)
        send("e", SB.at[rel(0, 1), 0:CUT], re, Y)

    def g_send():
        arrived("d2")

        def body(at):
            s, t = at(0), at(CUT)
            SB[rel(2, 0), t] = (T[rel(2, 0), t] + rd[2, s].astype(f32)).astype(bf16)

        rows_loop(ROWS - CUT, body)
        send("gp", SB.at[rel(2, 0), CUT:MID2], rgp, XP)
        send("gm", SB.at[rel(2, 0), MID2:ROWS], rgm, XM)

    def h_send():
        arrived("d1", "d3", "gp", "gm")
        half = MID2 - CUT

        def body(at):
            s, u, t, v = at(0), at(half), at(CUT), at(MID2)
            SB[rel(1, 0), t] = (T[rel(1, 0), t] + rd[1, s].astype(f32) + rgp[s].astype(f32)).astype(bf16)
            SB[rel(1, 0), v] = (T[rel(1, 0), v] + rd[1, u].astype(f32)).astype(bf16)
            SB[rel(3, 0), t] = (T[rel(3, 0), t] + rd[3, s].astype(f32)).astype(bf16)
            SB[rel(3, 0), v] = (T[rel(3, 0), v] + rd[3, u].astype(f32) + rgm[s].astype(f32)).astype(bf16)

        rows_loop(half, body)
        send("hp", SB.at[rel(1, 0), CUT:ROWS], rhp, XP)
        send("hm", SB.at[rel(3, 0), CUT:ROWS], rhm, XM)

    def finish_high():
        arrived("d0", "hp", "hm")

        def body(at):
            s, t = at(0), at(CUT)
            G[t] = T[rel(0, 0), t] + rd[0, s].astype(f32) + rhp[s].astype(f32) + rhm[s].astype(f32)

        rows_loop(ROWS - CUT, body)
        store(G.at[CUT:ROWS], grad_out.at[0, CUT:ROWS])

    def finish_low():
        arrived("cp0a", "cp0b", "cm0a", "cm0b")

        def body(at):
            s = at(0)
            G[s] = T[rel(0, 0), s] + rbp[0, s].astype(f32) + rbm[0, s].astype(f32)

        rows_loop(CUT, body)
        arrived("e")

        def body2(at):
            s = at(0)
            G[s] = G[s] + re[s].astype(f32)

        rows_loop(CUT, body2)
        store(G.at[0:CUT], grad_out.at[0, 0:CUT])

    def kv_part(slot, dst):
        for h in range(2):
            @pl.loop(0, 2)
            def _(j):
                cols = pl.ds(pl.multiple_of(h * 512 + j * 256, 256), 256)
                weights = Wb[:, :, cols].reshape(HALF, 256)
                dst[:, cols] = jnp.dot(Xb[slot], weights, preferred_element_type=f32)

            if slot == 1:
                cols = slice(h * 512, h * 512 + 512)
                send("kv%d" % h, KVs.at[:, cols], KVr.at[:, cols], SIB)

    def kv_compute():
        load_w.wait()
        arrived("yP2_0", "yP2_1", "yP2_3", "yP2_2a", "yP2_2b", "xpfP1", "xmfP1", "xpfQ1", "xmfQ1")
        kv_part(1, KVs)
        kv_part(0, KVo)

    def kv_finish():
        arrived("kv0", "kv1")

        def body(at):
            s = at(0)
            KVb[s] = (KVo[s] + KVr[s]).astype(bf16)

        rows_loop(TOK, body)
        store(KVb, kv_out)

    own_term(rel(1, 1))
    own_term(rel(3, 1))
    z3()
    arrived("cs", "xs%d" % rel(2, 0), "xs%d" % rel(2, 1))
    both_terms(rel(2, 0))
    both_terms(rel(2, 1))
    b_send(0)
    b_send(1)
    d_send(2)
    a_p2()
    a_q1()
    own_term(rel(1, 0))
    own_term(rel(3, 0))
    arrived(*["xs%d" % rel(dx, dy) for dx, dy in ((1, 1), (3, 1), (1, 0), (3, 0), (0, 1), (0, 0))])
    for dx, dy in ((1, 1), (3, 1), (1, 0), (3, 0)):
        both_terms(rel(dx, dy))
        c_plain(dx, dy)
        if dy == 1:
            d_send(dx)
    a_p1()
    z2()
    own_term(rel(0, 1))
    own_term(rel(0, 0))
    both_terms(rel(0, 1))
    d_send(0)
    both_terms(rel(0, 0))
    a_p2far()
    z1()
    a_fq1()
    c_added(1)
    c_added(0)
    g_send()
    z0()
    outer_step()
    kv_compute()
    g1()
    h_send()
    e_send()
    g2()
    kv_finish()
    g3()
    finish_high()
    g4()
    finish_low()
    g5()

    for cp in sent.values():
        cp.wait_send()
    for cp in stores:
        cp.wait()


def on_device(inputs, projection, cotangent, pseudo_grad, outer_params, outer_momentum):
    any_ = pl.BlockSpec(memory_space=pl.ANY)
    vm = pltpu.VMEM
    scratch = [
        vm((2, TOK, HALF), bf16),
        vm((2, TOK, KV), bf16),
        vm((8, ROWS, KV), bf16),
        vm((8, ROWS, KV), bf16),
        vm((8, ROWS, KV), f32),
        vm((8, ROWS, KV), bf16),
        vm((TOK, KV), f32),
        vm((TOK, KV), f32),
        vm((TOK, KV), f32),
        vm((TOK, KV), bf16),
        vm((2, MID1, KV), bf16),
        vm((2, MID1, KV), bf16),
        vm((4, ROWS - CUT, KV), bf16),
        vm((2, CUT, KV), bf16),
        vm((2, CUT, KV), bf16),
        vm((CUT, KV), bf16),
        vm((MID2 - CUT, KV), bf16),
        vm((MID2 - CUT, KV), bf16),
        vm((ROWS - CUT, KV), bf16),
        vm((ROWS - CUT, KV), bf16),
        vm((ROWS, KV), f32),
        vm((8, 2, FR, FC), bf16),
        vm((FR, FC), bf16),
        vm((FR, FC), bf16),
        vm((2, 3, 2, FR, FC), f32),
        vm((2, 3, 2, FR, FC), f32),
        vm((2, FR, FC), f32),
        vm((FR, FC), f32),
        vm((FR, FC), f32),
        vm((FR, FC), f32),
        vm((FR, FC), f32),
        vm((FR, FC), f32),
        vm((8, 2, FR, FC), bf16),
        pltpu.SemaphoreType.DMA((len(MESSAGES),)),
        pltpu.SemaphoreType.DMA((len(MESSAGES),)),
        pltpu.SemaphoreType.DMA((64,)),
    ]
    return pl.pallas_call(
        kernel,
        out_shape=(
            jax.ShapeDtypeStruct((TOK, KV), bf16),
            jax.ShapeDtypeStruct((1, ROWS, KV), f32),
            jax.ShapeDtypeStruct((FR, FC), f32),
            jax.ShapeDtypeStruct((FR, FC), f32),
            jax.ShapeDtypeStruct((FR, D), bf16),
        ),
        in_specs=[any_] * 6,
        out_specs=(any_,) * 5,
        scratch_shapes=scratch,
        compiler_params=pltpu.CompilerParams(
            collective_id=0, has_side_effects=True, vmem_limit_bytes=60 * 2**20
        ),
        cost_estimate=pl.CostEstimate(flops=6 * 10**9, bytes_accessed=3 * 10**7, transcendentals=0),
    )(inputs, projection, cotangent, pseudo_grad, outer_params, outer_momentum)


def solution(mesh):
    return jax.shard_map(
        on_device,
        mesh=mesh,
        in_specs=(
            P(("replica", "fsdp"), None),
            P("replica", "fsdp", None),
            P(("replica", "fsdp"), None),
            P("replica", "fsdp", None),
            P("fsdp", "replica"),
            P("fsdp", "replica"),
        ),
        out_specs=(
            P(("replica", "fsdp"), None),
            P("replica", "fsdp", None),
            P("fsdp", "replica"),
            P("fsdp", "replica"),
            P("fsdp", None),
        ),
        check_vma=False,
    )
```

time: 540 us -> 85.7 us (0.16)
  waiting for transfers between devices: 489 us -> 0 us
  Pallas kernels: 0 us -> 78.2 us
  other arithmetic: 18.7 us -> 0 us
  matrix products: 14.6 us -> 0 us
  between operations: 13.8 us -> 0.67 us
  local copies, waits for them, and re-layouts: 0.73 us -> 6.76 us
    all_gather x3 -> x0, waiting for transfers between devices: 213 us -> none  [the longest x1 71.6 us: on_device(): lax.all_gather(weight_shard, 'fsdp', axis=0, tiled=True)]
    reduce_scatter x1 -> x0, waiting for transfers between devices: 151 us -> none  [on_device(): lax.psum_scatter(lax.optimization_barrier(partial_term.astype(jnp.bfloat1...]
    psum x1 -> x0, waiting for transfers between devices: 123 us -> none  [on_device(): summed = lax.psum(local_delta, 'replica')]
    pallas_call x0 -> x1, Pallas kernels: none -> 78.2 us  [on_device(): pl.pallas_call(kernel, out_shape=(jax.ShapeDtypeStruct((TOK, KV), bf16),...]
    convert_element_type x3 -> x0, other arithmetic: 18.7 us -> none  [the longest x1 11.3 us: on_device(): lax.optimization_barrier(partial_term.astype(jnp.bfloat16))]
    dot_general x2 -> x0, matrix products: 14.6 us -> none  [the longest x1 7.85 us: on_device(): jnp.einsum('td,tc->dc', columns, cotangent, preferred_element_type=jnp.fl...]
    unnamed x2 -> x11, local copies, waits for them, and re-layouts: 0.01 us -> 6.76 us
  transfers between devices with their start and end apart: 5 -> 0, of which waited for: 5 -> 0; matrix products, arithmetic and copies ran while one was open for 6% -> 0% of each run, Pallas kernels for 0% -> 0%
where the time goes in v1:
time: 85.7 us; the launch traced here: 85.6 us
  Pallas kernels  78.2 us (91%)
  local copies, waits for them, and re-layouts  6.76 us (8%)
    pallas_call x1, Pallas kernels, on_device(): pl.pallas_call(kernel, out_shape=(jax.ShapeDtypeStruct((TOK, KV), bf16),...  78.2 us
    unnamed x11, local copies, waits for them, and re-layouts  6.76 us

profile of v1, /device:TPU:24, one launch (start us, length us, event | category | flops | bytes accessed | tf_op | source)
XLA Modules:
  0.0 85.6 jit_solution(747674422720104146)
XLA Ops:
  0.6 78.2 %shard_map.101 = (bf16[384,1024]{1,0:T(8,128)(2,1)}, f32[1,256,1024]{2,1,0:T(8,128)}, f32[128,256]{1,0:T(8,128)}, f32[128,256]{1,0:T(8,128)}, bf16[128,4096]{1,0:T(8,128)(2,1)}) custom-call(bf16[384,4096]{1,0:T(8,128)(2,1)} %x_hbm.1, bf16[1,256,1024]{2,1,0:T(8,128)(2,1)} %w_hbm.1, bf16[384,1024]{1,0:T(8,128)(2,1)} %c_hbm.1, bf16[1,128,4096]{2,1,0:T(8,128)(2,1)} %ps_hbm.1, ...), custom_call_target="tpu_custom_call" | custom-call | flops 6000000000 | bytes 30000000 | tf_op jit(solution)/shard_map/pallas_call | solution.py:516
  78.8 0.0 copy-start.2
  78.8 0.0 copy-start.1
  78.8 0.0 copy-start
  78.8 2.2 %copy.16 = bf16[384,1024]{1,0:T(8,128)(2,1)} copy(bf16[384,1024]{1,0:T(8,128)(2,1)} %get-tuple-element.10) | data formatting | bytes 1572864
  81.0 2.3 %copy.17 = f32[1,256,1024]{2,1,0:T(8,128)} copy(f32[1,256,1024]{2,1,0:T(8,128)} %get-tuple-element.11) | data formatting | bytes 2097152
  83.3 0.0 copy-done.2
  83.3 0.7 copy.18
  84.0 0.0 copy-done.1
  84.0 0.7 copy.19
  84.6 0.0 copy-done
  84.6 1.0 %copy.20 = bf16[128,4096]{1,0:T(8,128)(2,1)} copy(bf16[128,4096]{1,0:T(8,128)(2,1)S(1)} %copy-done) | data formatting | bytes 2097152
Async XLA Ops:
  78.8 4.5 %copy-start.2 = (f32[128,256]{1,0:T(8,128)S(1)}, f32[128,256]{1,0:T(8,128)}, u32[]{:S(2)}) copy-start(f32[128,256]{1,0:T(8,128)} %get-tuple-element.12) | copy-start | bytes 393220
  78.8 5.2 %copy-start.1 = (f32[128,256]{1,0:T(8,128)S(1)}, f32[128,256]{1,0:T(8,128)}, u32[]{:S(2)}) copy-start(f32[128,256]{1,0:T(8,128)} %get-tuple-element.13) | copy-start | bytes 393220
  78.8 5.8 %copy-start = (bf16[128,4096]{1,0:T(8,128)(2,1)S(1)}, bf16[128,4096]{1,0:T(8,128)(2,1)}, u32[]{:S(2)}) copy-start(bf16[128,4096]{1,0:T(8,128)(2,1)} %get-tuple-element.14) | copy-start | bytes 3145732

commit v2 on v1

--- a/solution.py
+++ b/solution.py
@@ -45,10 +45,10 @@
 
 def kernel(
     x_hbm, w_hbm, c_hbm, ps_hbm, op_hbm, om_hbm,
-    kv_out, grad_out, np_out, nm_out, lw_out,
-    Xb, Cb, Wb, TO, T, SB, KVs, KVo, KVr, KVb,
-    rap, ram, rd, rbp, rbm, re, rgp, rgm, rhp, rhm, G,
-    PSb, zq4p, zq4m, zs, zq, ZS, yr, OPb, OMb, NP, NM, LW,
+    KVb, G, NP, NM, LW,
+    Xb, Cb, Wb, TO, T, SB, KVs, KVo, KVr,
+    rap, ram, rd, rbp, rbm, re, rgp, rgm, rhp, rhm,
+    PSb, zq4p, zq4m, zs, zq, ZS, yr, OPb, OMb,
     ssem, rsem, lsem,
 ):
     r_id = lax.axis_index("replica")
@@ -213,18 +213,6 @@
         rows_loop(FR, body)
         send("yo", ZS.at[1 - ylo], yr, YL)
 
-    stores = []
-
-    def store(src, dst):
-        cp = pltpu.make_async_copy(src, dst, lsem.at[len(locals_) + len(stores)])
-        cp.start()
-        stores.append(cp)
-
-    def store_lw(dz, blocks=(0, 1)):
-        for b in blocks:
-            cols = pl.ds(pl.multiple_of(b * HALF + lax.rem(z + dz, 8) * FC, FC), FC)
-            store(LW.at[dz, b], lw_out.at[:, cols])
-
     def outer_step():
         for cp in load_o:
             cp.wait()
@@ -241,39 +229,29 @@
 
         rows_loop(FR, body)
         send("yl", LW.at[0, ylo], LW.at[0, ylo], YL)
-        store(NM, nm_out)
-        store(NP, np_out)
 
     def g1():
         arrived("yl")
         send("gp1", LW.at[0], LW.at[7], ZP)
         send("gm1", LW.at[0], LW.at[1], ZM)
-        store_lw(0)
 
     def g2():
         arrived("gp1", "gm1")
         send("gp2", LW.at[7], LW.at[6], ZP)
         send("gm2", LW.at[1], LW.at[2], ZM)
-        store_lw(7)
-        store_lw(1)
 
     def g3():
         arrived("gp2", "gm2")
         send("gp3", LW.at[6], LW.at[5], ZP)
         send("gm3", LW.at[2], LW.at[3], ZM)
-        store_lw(6)
-        store_lw(2)
 
     def g4():
         arrived("gp3", "gm3")
         send("gp4", LW.at[5, 0], LW.at[4, 0], ZP)
         send("gm4", LW.at[3, 1], LW.at[4, 1], ZM)
-        store_lw(5)
-        store_lw(3)
 
     def g5():
         arrived("gp4", "gm4")
-        store_lw(4)
 
     def a_p2():
         arrived("xpP2", "xmP2")
@@ -373,7 +351,6 @@
             G[t] = T[rel(0, 0), t] + rd[0, s].astype(f32) + rhp[s].astype(f32) + rhm[s].astype(f32)
 
         rows_loop(ROWS - CUT, body)
-        store(G.at[CUT:ROWS], grad_out.at[0, CUT:ROWS])
 
     def finish_low():
         arrived("cp0a", "cp0b", "cm0a", "cm0b")
@@ -390,7 +367,6 @@
             G[s] = G[s] + re[s].astype(f32)
 
         rows_loop(CUT, body2)
-        store(G.at[0:CUT], grad_out.at[0, 0:CUT])
 
     def kv_part(slot, dst):
         for h in range(2):
@@ -404,11 +380,9 @@
                 cols = slice(h * 512, h * 512 + 512)
                 send("kv%d" % h, KVs.at[:, cols], KVr.at[:, cols], SIB)
 
-    def kv_compute():
+    def kv_wait():
         load_w.wait()
         arrived("yP2_0", "yP2_1", "yP2_3", "yP2_2a", "yP2_2b", "xpfP1", "xmfP1", "xpfQ1", "xmfQ1")
-        kv_part(1, KVs)
-        kv_part(0, KVo)
 
     def kv_finish():
         arrived("kv0", "kv1")
@@ -418,62 +392,80 @@
             KVb[s] = (KVo[s] + KVr[s]).astype(bf16)
 
         rows_loop(TOK, body)
-        store(KVb, kv_out)
 
     own_term(rel(1, 1))
     own_term(rel(3, 1))
     z3()
-    arrived("cs", "xs%d" % rel(2, 0), "xs%d" % rel(2, 1))
-    both_terms(rel(2, 0))
-    both_terms(rel(2, 1))
-    b_send(0)
-    b_send(1)
-    d_send(2)
-    a_p2()
-    a_q1()
     own_term(rel(1, 0))
     own_term(rel(3, 0))
-    arrived(*["xs%d" % rel(dx, dy) for dx, dy in ((1, 1), (3, 1), (1, 0), (3, 0), (0, 1), (0, 0))])
-    for dx, dy in ((1, 1), (3, 1), (1, 0), (3, 0)):
-        both_terms(rel(dx, dy))
-        c_plain(dx, dy)
-        if dy == 1:
-            d_send(dx)
-    a_p1()
-    z2()
+    arrived("cs", *["xs%d" % r for r in range(8)])
+    both_terms(rel(2, 1))
+    a_p2()
+    both_terms(rel(2, 0))
     own_term(rel(0, 1))
     own_term(rel(0, 0))
+    a_q1()
+    z2()
+    both_terms(rel(1, 1))
+    both_terms(rel(3, 1))
+    a_p1()
+    b_send(1)
+    a_p2far()
+    d_send(2)
+    both_terms(rel(1, 0))
+    both_terms(rel(3, 0))
     both_terms(rel(0, 1))
-    d_send(0)
     both_terms(rel(0, 0))
-    a_p2far()
     z1()
     a_fq1()
+    z0()
+    d_send(1)
     c_added(1)
+    c_plain(1, 1)
+    c_plain(3, 1)
+    b_send(0)
+    outer_step()
+    d_send(3)
+    g_send()
+    c_plain(1, 0)
+    c_plain(3, 0)
+    kv_wait()
+    kv_part(1, KVs)
+    g1()
+    kv_part(0, KVo)
+    e_send()
+    d_send(0)
+    g2()
     c_added(0)
-    g_send()
-    z0()
-    outer_step()
-    kv_compute()
-    g1()
     h_send()
-    e_send()
-    g2()
+    g3()
     kv_finish()
-    g3()
-    finish_high()
     g4()
     finish_low()
     g5()
+    finish_high()
 
     for cp in sent.values():
         cp.wait_send()
-    for cp in stores:
+
+
+def write_out(kv, grad, params, moment, weights, kv_out, grad_out, np_out, nm_out, lw_out, sem):
+    z = lax.rem(lax.axis_index("replica"), 8)
+    pairs = [(kv, kv_out), (grad, grad_out.at[0]), (params, np_out), (moment, nm_out)]
+    for dz in range(8):
+        for b in range(2):
+            cols = pl.ds(pl.multiple_of(b * HALF + lax.rem(z + dz, 8) * FC, FC), FC)
+            pairs.append((weights.at[dz, b], lw_out.at[:, cols]))
+    copies = [pltpu.make_async_copy(src, dst, sem.at[i]) for i, (src, dst) in enumerate(pairs)]
+    for cp in copies:
+        cp.start()
+    for cp in copies:
         cp.wait()
 
 
 def on_device(inputs, projection, cotangent, pseudo_grad, outer_params, outer_momentum):
     any_ = pl.BlockSpec(memory_space=pl.ANY)
+    inside = pl.BlockSpec(memory_space=pltpu.VMEM)
     vm = pltpu.VMEM
     scratch = [
         vm((2, TOK, HALF), bf16),
@@ -485,7 +477,6 @@
         vm((TOK, KV), f32),
         vm((TOK, KV), f32),
         vm((TOK, KV), f32),
-        vm((TOK, KV), bf16),
         vm((2, MID1, KV), bf16),
         vm((2, MID1, KV), bf16),
         vm((4, ROWS - CUT, KV), bf16),
@@ -496,7 +487,6 @@
         vm((MID2 - CUT, KV), bf16),
         vm((ROWS - CUT, KV), bf16),
         vm((ROWS - CUT, KV), bf16),
-        vm((ROWS, KV), f32),
         vm((8, 2, FR, FC), bf16),
         vm((FR, FC), bf16),
         vm((FR, FC), bf16),
@@ -506,15 +496,32 @@
         vm((FR, FC), f32),
         vm((FR, FC), f32),
         vm((FR, FC), f32),
-        vm((FR, FC), f32),
-        vm((FR, FC), f32),
-        vm((8, 2, FR, FC), bf16),
         pltpu.SemaphoreType.DMA((len(MESSAGES),)),
         pltpu.SemaphoreType.DMA((len(MESSAGES),)),
         pltpu.SemaphoreType.DMA((64,)),
     ]
+    operands = (inputs, projection, cotangent, pseudo_grad, outer_params, outer_momentum)
+    operands = [pltpu.with_memory_space_constraint(a, pltpu.HBM) for a in operands]
+    results = pl.pallas_call(
+        kernel,
+        out_shape=(
+            vm((TOK, KV), bf16),
+            vm((ROWS, KV), f32),
+            vm((FR, FC), f32),
+            vm((FR, FC), f32),
+            vm((8, 2, FR, FC), bf16),
+        ),
+        in_specs=[any_] * 6,
+        out_specs=(inside,) * 5,
+        scratch_shapes=scratch,
+        compiler_params=pltpu.CompilerParams(
+            collective_id=0, has_side_effects=True, vmem_limit_bytes=44 * 2**20
+        ),
+        cost_estimate=pl.CostEstimate(flops=6 * 10**9, bytes_accessed=3 * 10**7, transcendentals=0),
+    )(*operands)
+    results = [pltpu.with_memory_space_constraint(a, pltpu.VMEM) for a in results]
     return pl.pallas_call(
-        kernel,
+        write_out,
         out_shape=(
             jax.ShapeDtypeStruct((TOK, KV), bf16),
             jax.ShapeDtypeStruct((1, ROWS, KV), f32),
@@ -522,14 +529,11 @@
             jax.ShapeDtypeStruct((FR, FC), f32),
             jax.ShapeDtypeStruct((FR, D), bf16),
         ),
-        in_specs=[any_] * 6,
+        in_specs=[inside] * 5,
         out_specs=(any_,) * 5,
-        scratch_shapes=scratch,
-        compiler_params=pltpu.CompilerParams(
-            collective_id=0, has_side_effects=True, vmem_limit_bytes=60 * 2**20
-        ),
-        cost_estimate=pl.CostEstimate(flops=6 * 10**9, bytes_accessed=3 * 10**7, transcendentals=0),
-    )(inputs, projection, cotangent, pseudo_grad, outer_params, outer_momentum)
+        scratch_shapes=[pltpu.SemaphoreType.DMA((20,))],
+        compiler_params=pltpu.CompilerParams(vmem_limit_bytes=44 * 2**20),
+    )(*results)
 
 
 def solution(mesh):

time: 85.7 us -> 69.9 us (0.82); the launches traced: 85.6 us -> 68.7 us
  Pallas kernels: 78.2 us -> 68 us
  local copies, waits for them, and re-layouts: 6.76 us -> 0 us
    pallas_call x1 -> x2, Pallas kernels: 78.2 us -> 68 us  [the longest x1 66.2 us: on_device(): pl.pallas_call(kernel, out_shape=(vm((TOK, KV), bf16), vm((ROWS, KV), f32...]
    unnamed x11 -> x0, local copies, waits for them, and re-layouts: 6.76 us -> none
where the time goes in v2:
time: 69.9 us; the launch traced here: 68.7 us
  Pallas kernels  68 us (97%)
    pallas_call x1, Pallas kernels, on_device(): pl.pallas_call(kernel, out_shape=(vm((TOK, KV), bf16), vm((ROWS, KV), f32...  66.2 us
    pallas_call x1, Pallas kernels, on_device(): pl.pallas_call(write_out, out_shape=(jax.ShapeDtypeStruct((TOK, KV), bf16...  1.82 us

profile of v2, /device:TPU:24, one launch (start us, length us, event | category | flops | bytes accessed | tf_op | source)
XLA Modules:
  0.0 68.7 jit_solution(12956166466678531048)
XLA Ops:
  0.6 66.2 %shard_map.101 = (bf16[384,1024]{1,0:T(8,128)(2,1)S(1)}, f32[256,1024]{1,0:T(8,128)S(1)}, f32[128,256]{1,0:T(8,128)S(1)}, f32[128,256]{1,0:T(8,128)S(1)}, bf16[8,2,128,256]{3,2,1,0:T(8,128)(2,1)S(1)}) custom-call(bf16[384,4096]{1,0:T(8,128)(2,1)} %x_hbm.1, bf16[1,256,1024]{2,1,0:T(8,128)(2,1)} %w_hbm.1, bf16[384,1024]{1,0:T(8,128)(2,1)} %c_hbm.1, ...), custom_call_target="tpu_custom_call" | custom-call | flops 6000000000 | bytes 30000000 | tf_op jit(solution)/shard_map/pallas_call | solution.py:505
  66.9 1.8 %shard_map.102 = (bf16[384,1024]{1,0:T(8,128)(2,1)}, f32[1,256,1024]{2,1,0:T(8,128)}, f32[128,256]{1,0:T(8,128)}, f32[128,256]{1,0:T(8,128)}, bf16[128,4096]{1,0:T(8,128)(2,1)}) custom-call(bf16[384,1024]{1,0:T(8,128)(2,1)S(1)} %get-tuple-element.10.kv, f32[256,1024]{1,0:T(8,128)S(1)} %get-tuple-element.11.grad, f32[128,256]{1,0:T(8,128)S(1)} %get-tuple-element.12.params, ...), custom_call_target="tpu_custom_call" | custom-call | tf_op jit(solution)/shard_map/pallas_call | solution.py:523

commit v3 on v2

--- a/solution.py
+++ b/solution.py
@@ -32,9 +32,10 @@
     + ["c%s%d%s" % (d, y, h) for d in "pm" for y in (0, 1) for h in "ab"]
     + ["d%d" % x for x in range(4)]
     + ["e", "gp", "gm", "hp", "hm"]
-    + ["z%s%d" % (d, k) for d in "pm" for k in (4, 3, 2, 1)]
+    + ["z%s%s" % (d, k) for d in "pm" for k in ("L4", "S3", "L3", "S2", "L2", "S1", "L1")]
     + ["yo", "yl"]
-    + ["g%s%d" % (d, k) for d in "pm" for k in (1, 2, 3, 4)]
+    + ["g%s%s%d" % (d, k, n) for d in "pm" for k in "oq" for n in (1, 2, 3)]
+    + ["gpo4", "gmq4"]
 )
 NUMBER = {name: i for i, name in enumerate(MESSAGES)}
 
@@ -48,8 +49,8 @@
     KVb, G, NP, NM, LW,
     Xb, Cb, Wb, TO, T, SB, KVs, KVo, KVr,
     rap, ram, rd, rbp, rbm, re, rgp, rgm, rhp, rhm,
-    PSb, zq4p, zq4m, zs, zq, ZS, yr, OPb, OMb,
-    ssem, rsem, lsem,
+    PSb, zraw, zout, zin, ZS, yr, OPb, OMb,
+    ssem, rsem, lsem, zsem,
 ):
     r_id = lax.axis_index("replica")
     f_id = lax.axis_index("fsdp")
@@ -71,8 +72,13 @@
     SIB = device(x, yh, z, ylo, 1 - c)
 
     barrier = pltpu.get_barrier_semaphore()
-    for dev in (XP, XM, Y, YL, ZP, ZM, SIB):
+    for dev in (XP, XM, Y, YL, SIB):
         pl.semaphore_signal(barrier, inc=1, device_id=dev, device_id_type=MESH)
+
+    @pl.when(c == 0)
+    def _():
+        for dev in (ZP, ZM):
+            pl.semaphore_signal(barrier, inc=1, device_id=dev, device_id_type=MESH)
 
     def columns(r, core):
         chip = (yh if r < 4 else 1 - yh) * 4 + lax.rem(x + r % 4, 4)
@@ -110,9 +116,13 @@
         cp.start()
         sent[name] = cp
 
+    here = set()
+
     def arrived(*names):
         for name in names:
-            sent[name].wait_recv()
+            if name not in here:
+                here.add(name)
+                sent[name].wait_recv()
 
     def rows_loop(n, body):
         @pl.loop(0, n // 16)
@@ -130,6 +140,8 @@
             ).astype(bf16)
 
     def both_terms(r):
+        arrived("cs", "xs%d" % r)
+
         @pl.loop(0, 2)
         def _(j):
             cols = pl.ds(pl.multiple_of(j * 512, 512), 512)
@@ -146,7 +158,15 @@
     own_term(rel(2, 0))
     own_term(rel(2, 1))
 
-    pl.semaphore_wait(barrier, 7)
+    @pl.when(c == 0)
+    def _():
+        pl.semaphore_wait(barrier, 7)
+        for i, dev in enumerate((ZP, ZM)):
+            pl.semaphore_signal(zsem.at[i], inc=1, device_id=dev, device_id_type=MESH)
+
+    @pl.when(c == 1)
+    def _():
+        pl.semaphore_wait(barrier, 5)
 
     send("xpP2", w_hbm.at[0, CUT:ROWS], Wb.at[rel(3, 0), CUT:ROWS], XP)
     send("xmP2", w_hbm.at[0, CUT:ROWS], Wb.at[rel(1, 0), CUT:ROWS], XM)
@@ -154,61 +174,55 @@
     send("cs", c_hbm, Cb.at[1], SIB)
     for r in (rel(2, 0), rel(2, 1), rel(1, 1), rel(3, 1), rel(1, 0), rel(3, 0), rel(0, 1), rel(0, 0)):
         send("xs%d" % r, x_hbm.at[:, columns(r, 1 - c)], Xb.at[1, :, lanes(r)], SIB)
-    for cp in load_ps:
-        cp.wait()
-    send("zp4", PSb.at[4, 0], zq4p, ZP)
-    send("zm4", PSb.at[4, 1], zq4m, ZM)
     send("xpP1", w_hbm.at[0, 0:CUT], Wb.at[rel(3, 0), 0:CUT], XP)
     send("xmP1", w_hbm.at[0, 0:CUT], Wb.at[rel(1, 0), 0:CUT], XM)
     send("yP2_0", w_hbm.at[0, CUT:ROWS], Wb.at[rel(0, 1), CUT:ROWS], Y)
 
-    def z3():
-        arrived("zp4", "zm4")
-
-        def body(at):
-            s = at(0)
-            zs[0, 0, 0, s] = PSb[3, 0, s].astype(f32) + zq4p[s].astype(f32)
-            zs[0, 0, 1, s] = PSb[3, 1, s].astype(f32)
-            zs[1, 0, 0, s] = PSb[5, 0, s].astype(f32)
-            zs[1, 0, 1, s] = PSb[5, 1, s].astype(f32) + zq4m[s].astype(f32)
+    def z_start():
+        for cp in load_ps:
+            cp.wait()
+
+        @pl.when(c == 0)
+        def _():
+            for i in range(2):
+                pl.semaphore_wait(zsem.at[i], 1)
+            pl.semaphore_signal(zsem.at[2], inc=1, device_id=SIB, device_id_type=MESH)
+
+        @pl.when(c == 1)
+        def _():
+            pl.semaphore_wait(zsem.at[2], 1)
+
+        send("zpL4", PSb.at[4, 0], zraw.at[0, 0], ZP)
+        send("zmL4", PSb.at[4, 1], zraw.at[0, 1], ZM)
+        send("zpS3", PSb.at[3, 1], zraw.at[1, 0], ZP)
+        send("zmS3", PSb.at[5, 0], zraw.at[1, 1], ZM)
+
+    STAGES = ("L3", "S2", "L2", "S1", "L1")
+
+    def ring(stage, before, terms):
+        arrived("zp" + before, "zm" + before)
+        k = STAGES.index(stage)
+
+        def body(at):
+            s = at(0)
+            for way, (dz, b) in enumerate(terms):
+                if before in STAGES:
+                    come = zin[STAGES.index(before), way, s]
+                else:
+                    come = zraw[("L4", "S3").index(before), way, s].astype(f32)
+                zout[k, way, s] = PSb[dz, b, s].astype(f32) + come
 
         rows_loop(FR, body)
-        send("zp3", zs.at[0, 0], zq.at[0, 0], ZP)
-        send("zm3", zs.at[1, 0], zq.at[1, 0], ZM)
-
-    def z2():
-        arrived("zp3", "zm3")
-
-        def body(at):
-            s = at(0)
-            for b in range(2):
-                zs[0, 1, b, s] = PSb[2, b, s].astype(f32) + zq[0, 0, b, s]
-                zs[1, 1, b, s] = PSb[6, b, s].astype(f32) + zq[1, 0, b, s]
-
-        rows_loop(FR, body)
-        send("zp2", zs.at[0, 1], zq.at[0, 1], ZP)
-        send("zm2", zs.at[1, 1], zq.at[1, 1], ZM)
-
-    def z1():
-        arrived("zp2", "zm2")
-
-        def body(at):
-            s = at(0)
-            for b in range(2):
-                zs[0, 2, b, s] = PSb[1, b, s].astype(f32) + zq[0, 1, b, s]
-                zs[1, 2, b, s] = PSb[7, b, s].astype(f32) + zq[1, 1, b, s]
-
-        rows_loop(FR, body)
-        send("zp1", zs.at[0, 2], zq.at[0, 2], ZP)
-        send("zm1", zs.at[1, 2], zq.at[1, 2], ZM)
-
-    def z0():
-        arrived("zp1", "zm1")
-
-        def body(at):
-            s = at(0)
-            for b in range(2):
-                ZS[b, s] = PSb[0, b, s].astype(f32) + zq[0, 2, b, s] + zq[1, 2, b, s]
+        send("zp" + stage, zout.at[k, 0], zin.at[k, 0], ZP)
+        send("zm" + stage, zout.at[k, 1], zin.at[k, 1], ZM)
+
+    def z_total():
+        arrived("zpS1", "zmS1", "zpL1", "zmL1")
+
+        def body(at):
+            s = at(0)
+            ZS[0, s] = PSb[0, 0, s].astype(f32) + zin[4, 0, s] + zin[3, 1, s]
+            ZS[1, s] = PSb[0, 1, s].astype(f32) + zin[3, 0, s] + zin[4, 1, s]
 
         rows_loop(FR, body)
         send("yo", ZS.at[1 - ylo], yr, YL)
@@ -229,29 +243,19 @@
 
         rows_loop(FR, body)
         send("yl", LW.at[0, ylo], LW.at[0, ylo], YL)
-
-    def g1():
-        arrived("yl")
-        send("gp1", LW.at[0], LW.at[7], ZP)
-        send("gm1", LW.at[0], LW.at[1], ZM)
-
-    def g2():
-        arrived("gp1", "gm1")
-        send("gp2", LW.at[7], LW.at[6], ZP)
-        send("gm2", LW.at[1], LW.at[2], ZM)
-
-    def g3():
-        arrived("gp2", "gm2")
-        send("gp3", LW.at[6], LW.at[5], ZP)
-        send("gm3", LW.at[2], LW.at[3], ZM)
-
-    def g4():
-        arrived("gp3", "gm3")
-        send("gp4", LW.at[5, 0], LW.at[4, 0], ZP)
-        send("gm4", LW.at[3, 1], LW.at[4, 1], ZM)
-
-    def g5():
-        arrived("gp4", "gm4")
+        share("o", 1)
+
+    def share(which, n):
+        b = ylo if which == "o" else 1 - ylo
+        if n > 1:
+            arrived("gp%s%d" % (which, n - 1), "gm%s%d" % (which, n - 1))
+        elif which == "q":
+            arrived("yl")
+        up, down = (9 - n) % 8, n - 1
+        if n < 4 or which == "o":
+            send("gp%s%d" % (which, n), LW.at[up, b], LW.at[(up + 7) % 8, b], ZP)
+        if n < 4 or which == "q":
+            send("gm%s%d" % (which, n), LW.at[down, b], LW.at[(down + 1) % 8, b], ZM)
 
     def a_p2():
         arrived("xpP2", "xmP2")
@@ -368,20 +372,24 @@
 
         rows_loop(CUT, body2)
 
-    def kv_part(slot, dst):
-        for h in range(2):
-            @pl.loop(0, 2)
-            def _(j):
-                cols = pl.ds(pl.multiple_of(h * 512 + j * 256, 256), 256)
-                weights = Wb[:, :, cols].reshape(HALF, 256)
-                dst[:, cols] = jnp.dot(Xb[slot], weights, preferred_element_type=f32)
-
-            if slot == 1:
-                cols = slice(h * 512, h * 512 + 512)
-                send("kv%d" % h, KVs.at[:, cols], KVr.at[:, cols], SIB)
+    def kv_half(slot, h):
+        kv_wait()
+        dst = KVs if slot == 1 else KVo
+
+        @pl.loop(0, 2)
+        def _(j):
+            cols = pl.ds(pl.multiple_of(h * 512 + j * 256, 256), 256)
+            weights = Wb[:, :, cols].reshape(HALF, 256)
+            dst[:, cols] = jnp.dot(Xb[slot], weights, preferred_element_type=f32)
+
+        if slot == 1:
+            cols = slice(h * 512, h * 512 + 512)
+            send("kv%d" % h, KVs.at[:, cols], KVr.at[:, cols], SIB)
 
     def kv_wait():
-        load_w.wait()
+        if "w" not in here:
+            here.add("w")
+            load_w.wait()
         arrived("yP2_0", "yP2_1", "yP2_3", "yP2_2a", "yP2_2b", "xpfP1", "xmfP1", "xpfQ1", "xmfQ1")
 
     def kv_finish():
@@ -393,57 +401,63 @@
 
         rows_loop(TOK, body)
 
-    own_term(rel(1, 1))
-    own_term(rel(3, 1))
-    z3()
-    own_term(rel(1, 0))
-    own_term(rel(3, 0))
-    arrived("cs", *["xs%d" % r for r in range(8)])
-    both_terms(rel(2, 1))
+    z_start()
+    own_term(4)
+    own_term(7)
+    both_terms(6)
+    ring("L3", "L4", ((3, 0), (5, 1)))
+    own_term(5)
     a_p2()
-    both_terms(rel(2, 0))
-    own_term(rel(0, 1))
-    own_term(rel(0, 0))
+    ring("S2", "S3", ((2, 1), (6, 0)))
+    both_terms(2)
+    both_terms(5)
+    b_send(1)
+    both_terms(7)
+    ring("L2", "L3", ((2, 0), (6, 1)))
     a_q1()
-    z2()
-    both_terms(rel(1, 1))
-    both_terms(rel(3, 1))
-    a_p1()
-    b_send(1)
-    a_p2far()
-    d_send(2)
-    both_terms(rel(1, 0))
-    both_terms(rel(3, 0))
-    both_terms(rel(0, 1))
-    both_terms(rel(0, 0))
-    z1()
-    a_fq1()
-    z0()
-    d_send(1)
-    c_added(1)
+    own_term(1)
+    ring("S1", "S2", ((1, 1), (7, 0)))
+    ring("L1", "L2", ((1, 0), (7, 1)))
     c_plain(1, 1)
     c_plain(3, 1)
+    a_p1()
     b_send(0)
+    d_send(2)
+    z_total()
+    own_term(0)
+    c_added(1)
+    both_terms(1)
+    a_fq1()
+    d_send(1)
+    both_terms(4)
     outer_step()
+    own_term(3)
+    a_p2far()
+    g_send()
+    share("q", 1)
     d_send(3)
-    g_send()
+    share("o", 2)
+    both_terms(3)
+    e_send()
+    share("q", 2)
+    both_terms(0)
+    c_added(0)
     c_plain(1, 0)
     c_plain(3, 0)
-    kv_wait()
-    kv_part(1, KVs)
-    g1()
-    kv_part(0, KVo)
-    e_send()
+    share("o", 3)
+    kv_half(0, 0)
+    kv_half(1, 0)
     d_send(0)
-    g2()
-    c_added(0)
     h_send()
-    g3()
+    share("q", 3)
+    share("o", 4)
+    kv_half(1, 1)
+    share("q", 4)
+    kv_half(0, 1)
+    finish_low()
     kv_finish()
-    g4()
-    finish_low()
-    g5()
     finish_high()
+    arrived("gpo4", "gmq4")
 
     for cp in sent.values():
         cp.wait_send()
@@ -488,17 +502,17 @@
         vm((ROWS - CUT, KV), bf16),
         vm((ROWS - CUT, KV), bf16),
         vm((8, 2, FR, FC), bf16),
-        vm((FR, FC), bf16),
-        vm((FR, FC), bf16),
-        vm((2, 3, 2, FR, FC), f32),
-        vm((2, 3, 2, FR, FC), f32),
+        vm((2, 2, FR, FC), bf16),
+        vm((5, 2, FR, FC), f32),
+        vm((5, 2, FR, FC), f32),
         vm((2, FR, FC), f32),
         vm((FR, FC), f32),
         vm((FR, FC), f32),
         vm((FR, FC), f32),
         pltpu.SemaphoreType.DMA((len(MESSAGES),)),
         pltpu.SemaphoreType.DMA((len(MESSAGES),)),
-        pltpu.SemaphoreType.DMA((64,)),
+        pltpu.SemaphoreType.DMA((32,)),
+        pltpu.SemaphoreType.REGULAR((3,)),
     ]
     operands = (inputs, projection, cotangent, pseudo_grad, outer_params, outer_momentum)
     operands = [pltpu.with_memory_space_constraint(a, pltpu.HBM) for a in operands]

time: 69.9 us -> 66.3 us (0.948); the launches traced: 68.7 us -> 66.2 us
  Pallas kernels: 68 us -> 65.6 us
    pallas_call x1, Pallas kernels: 66.2 us -> 63.7 us  [on_device(): pl.pallas_call(kernel, out_shape=(vm((TOK, KV), bf16), vm((ROWS, KV), f32...]
where the time goes in v3:
time: 66.3 us; the launch traced here: 66.2 us
  Pallas kernels  65.6 us (99%)
    pallas_call x1, Pallas kernels, on_device(): pl.pallas_call(kernel, out_shape=(vm((TOK, KV), bf16), vm((ROWS, KV), f32...  63.7 us
    pallas_call x1, Pallas kernels, on_device(): pl.pallas_call(write_out, out_shape=(jax.ShapeDtypeStruct((TOK, KV), bf16...  1.82 us

profile of v3, /device:TPU:24, one launch (start us, length us, event | category | flops | bytes accessed | tf_op | source)
XLA Modules:
  0.0 66.2 jit_solution(16010231334988637719)
XLA Ops:
  0.6 63.7 %shard_map.101 = (bf16[384,1024]{1,0:T(8,128)(2,1)S(1)}, f32[256,1024]{1,0:T(8,128)S(1)}, f32[128,256]{1,0:T(8,128)S(1)}, f32[128,256]{1,0:T(8,128)S(1)}, bf16[8,2,128,256]{3,2,1,0:T(8,128)(2,1)S(1)}) custom-call(bf16[384,4096]{1,0:T(8,128)(2,1)} %x_hbm.1, bf16[1,256,1024]{2,1,0:T(8,128)(2,1)} %w_hbm.1, bf16[384,1024]{1,0:T(8,128)(2,1)} %c_hbm.1, ...), custom_call_target="tpu_custom_call" | custom-call | flops 6000000000 | bytes 30000000 | tf_op jit(solution)/shard_map/pallas_call | solution.py:519
  64.4 1.8 %shard_map.102 = (bf16[384,1024]{1,0:T(8,128)(2,1)}, f32[1,256,1024]{2,1,0:T(8,128)}, f32[128,256]{1,0:T(8,128)}, f32[128,256]{1,0:T(8,128)}, bf16[128,4096]{1,0:T(8,128)(2,1)}) custom-call(bf16[384,1024]{1,0:T(8,128)(2,1)S(1)} %get-tuple-element.10.kv, f32[256,1024]{1,0:T(8,128)S(1)} %get-tuple-element.11.grad, f32[128,256]{1,0:T(8,128)S(1)} %get-tuple-element.12.params, ...), custom_call_target="tpu_custom_call" | custom-call | tf_op jit(solution)/shard_map/pallas_call | solution.py:537

commit v4 on v3

--- a/solution.py
+++ b/solution.py
@@ -31,7 +31,7 @@
     + ["b%s%d" % (d, y) for d in "pm" for y in (0, 1)]
     + ["c%s%d%s" % (d, y, h) for d in "pm" for y in (0, 1) for h in "ab"]
     + ["d%d" % x for x in range(4)]
-    + ["e", "gp", "gm", "hp", "hm"]
+    + ["e", "gp", "gm", "hpa", "hpb", "hma", "hmb"]
     + ["z%s%s" % (d, k) for d in "pm" for k in ("L4", "S3", "L3", "S2", "L2", "S1", "L1")]
     + ["yo", "yl"]
     + ["g%s%s%d" % (d, k, n) for d in "pm" for k in "oq" for n in (1, 2, 3)]
@@ -50,7 +50,7 @@
     Xb, Cb, Wb, TO, T, SB, KVs, KVo, KVr,
     rap, ram, rd, rbp, rbm, re, rgp, rgm, rhp, rhm,
     PSb, zraw, zout, zin, ZS, yr, OPb, OMb,
-    ssem, rsem, lsem, zsem,
+    ssem, rsem, lsem, ready,
 ):
     r_id = lax.axis_index("replica")
     f_id = lax.axis_index("fsdp")
@@ -72,13 +72,20 @@
     SIB = device(x, yh, z, ylo, 1 - c)
 
     barrier = pltpu.get_barrier_semaphore()
-    for dev in (XP, XM, Y, YL, SIB):
-        pl.semaphore_signal(barrier, inc=1, device_id=dev, device_id_type=MESH)
-
-    @pl.when(c == 0)
-    def _():
-        for dev in (ZP, ZM):
-            pl.semaphore_signal(barrier, inc=1, device_id=dev, device_id_type=MESH)
+    NEAR = ("xp", "xm", "y", "yl", "zp", "zm", "sib")
+    device_of = dict(xp=XP, xm=XM, y=Y, yl=YL, zp=ZP, zm=ZM, sib=SIB)
+    first = dict(xp=x < 3, xm=x == 0, y=yh == 0, yl=ylo == 0, zp=z < 7, zm=z == 0, sib=c == 1)
+    back = dict(xp="xm", xm="xp", y="y", yl="yl", zp="zm", zm="zp", sib="sib")
+
+    for k in NEAR:
+        @pl.when(first[k])
+        def _():
+            pl.semaphore_signal(barrier, inc=1, device_id=device_of[k], device_id_type=MESH)
+
+    def gate(k):
+        @pl.when(first[k])
+        def _():
+            pl.semaphore_wait(ready.at[NEAR.index(k)], 1)
 
     def columns(r, core):
         chip = (yh if r < 4 else 1 - yh) * 4 + lax.rem(x + r % 4, 4)
@@ -152,49 +159,48 @@
             T[r, :, cols] = total
             SB[r, :, cols] = total.astype(bf16)
 
+    greeted = sum(jnp.where(first[k], 0, 1) for k in NEAR)
+
+    @pl.when(greeted > 0)
+    def _():
+        pl.semaphore_wait(barrier, greeted)
+
+    for k in NEAR:
+        @pl.when(jnp.logical_not(first[k]))
+        def _():
+            pl.semaphore_signal(
+                ready.at[NEAR.index(back[k])], inc=1, device_id=device_of[k], device_id_type=MESH
+            )
+
+    gate("xp")
+    send("xpP2", w_hbm.at[0, CUT:ROWS], Wb.at[rel(3, 0), CUT:ROWS], XP)
+    send("xpP1", w_hbm.at[0, 0:CUT], Wb.at[rel(3, 0), 0:CUT], XP)
+    gate("xm")
+    send("xmP2", w_hbm.at[0, CUT:ROWS], Wb.at[rel(1, 0), CUT:ROWS], XM)
+    send("xmP1", w_hbm.at[0, 0:CUT], Wb.at[rel(1, 0), 0:CUT], XM)
+    gate("y")
+    send("yP1", w_hbm.at[0, 0:CUT], Wb.at[rel(0, 1), 0:CUT], Y)
+    send("yP2_0", w_hbm.at[0, CUT:ROWS], Wb.at[rel(0, 1), CUT:ROWS], Y)
+    gate("sib")
+    send("cs", c_hbm, Cb.at[1], SIB)
+    for r in (rel(2, 0), rel(2, 1), rel(1, 1), rel(3, 1), rel(1, 0), rel(3, 0), rel(0, 1), rel(0, 0)):
+        send("xs%d" % r, x_hbm.at[:, columns(r, 1 - c)], Xb.at[1, :, lanes(r)], SIB)
+
     load_c.wait()
     for cp in load_x:
         cp.wait()
     own_term(rel(2, 0))
     own_term(rel(2, 1))
 
-    @pl.when(c == 0)
-    def _():
-        pl.semaphore_wait(barrier, 7)
-        for i, dev in enumerate((ZP, ZM)):
-            pl.semaphore_signal(zsem.at[i], inc=1, device_id=dev, device_id_type=MESH)
-
-    @pl.when(c == 1)
-    def _():
-        pl.semaphore_wait(barrier, 5)
-
-    send("xpP2", w_hbm.at[0, CUT:ROWS], Wb.at[rel(3, 0), CUT:ROWS], XP)
-    send("xmP2", w_hbm.at[0, CUT:ROWS], Wb.at[rel(1, 0), CUT:ROWS], XM)
-    send("yP1", w_hbm.at[0, 0:CUT], Wb.at[rel(0, 1), 0:CUT], Y)
-    send("cs", c_hbm, Cb.at[1], SIB)
-    for r in (rel(2, 0), rel(2, 1), rel(1, 1), rel(3, 1), rel(1, 0), rel(3, 0), rel(0, 1), rel(0, 0)):
-        send("xs%d" % r, x_hbm.at[:, columns(r, 1 - c)], Xb.at[1, :, lanes(r)], SIB)
-    send("xpP1", w_hbm.at[0, 0:CUT], Wb.at[rel(3, 0), 0:CUT], XP)
-    send("xmP1", w_hbm.at[0, 0:CUT], Wb.at[rel(1, 0), 0:CUT], XM)
-    send("yP2_0", w_hbm.at[0, CUT:ROWS], Wb.at[rel(0, 1), CUT:ROWS], Y)
-
     def z_start():
         for cp in load_ps:
             cp.wait()
 
-        @pl.when(c == 0)
-        def _():
-            for i in range(2):
-                pl.semaphore_wait(zsem.at[i], 1)
-            pl.semaphore_signal(zsem.at[2], inc=1, device_id=SIB, device_id_type=MESH)
-
-        @pl.when(c == 1)
-        def _():
-            pl.semaphore_wait(zsem.at[2], 1)
-
+        gate("zp")
         send("zpL4", PSb.at[4, 0], zraw.at[0, 0], ZP)
+        send("zpS3", PSb.at[3, 1], zraw.at[1, 0], ZP)
+        gate("zm")
         send("zmL4", PSb.at[4, 1], zraw.at[0, 1], ZM)
-        send("zpS3", PSb.at[3, 1], zraw.at[1, 0], ZP)
         send("zmS3", PSb.at[5, 0], zraw.at[1, 1], ZM)
 
     STAGES = ("L3", "S2", "L2", "S1", "L1")
@@ -225,6 +231,7 @@
             ZS[1, s] = PSb[0, 1, s].astype(f32) + zin[3, 0, s] + zin[4, 1, s]
 
         rows_loop(FR, body)
+        gate("yl")
         send("yo", ZS.at[1 - ylo], yr, YL)
 
     def outer_step():
@@ -344,17 +351,21 @@
             SB[rel(3, 0), v] = (T[rel(3, 0), v] + rd[3, u].astype(f32) + rgm[s].astype(f32)).astype(bf16)
 
         rows_loop(half, body)
-        send("hp", SB.at[rel(1, 0), CUT:ROWS], rhp, XP)
-        send("hm", SB.at[rel(3, 0), CUT:ROWS], rhm, XM)
-
-    def finish_high():
-        arrived("d0", "hp", "hm")
-
-        def body(at):
-            s, t = at(0), at(CUT)
+        send("hpa", SB.at[rel(1, 0), CUT:MID2], rhp.at[0:half], XP)
+        send("hma", SB.at[rel(3, 0), CUT:MID2], rhm.at[0:half], XM)
+        send("hpb", SB.at[rel(1, 0), MID2:ROWS], rhp.at[half : ROWS - CUT], XP)
+        send("hmb", SB.at[rel(3, 0), MID2:ROWS], rhm.at[half : ROWS - CUT], XM)
+
+    def finish_high(part):
+        arrived("d0", "hp" + part, "hm" + part)
+        half = MID2 - CUT
+        first = 0 if part == "a" else half
+
+        def body(at):
+            s, t = at(first), at(CUT + first)
             G[t] = T[rel(0, 0), t] + rd[0, s].astype(f32) + rhp[s].astype(f32) + rhm[s].astype(f32)
 
-        rows_loop(ROWS - CUT, body)
+        rows_loop(half, body)
 
     def finish_low():
         arrived("cp0a", "cp0b", "cm0a", "cm0b")
@@ -400,6 +411,14 @@
             KVb[s] = (KVo[s] + KVr[s]).astype(bf16)
 
         rows_loop(TOK, body)
+
+    done = set()
+
+    def all_sent(*later):
+        for name, cp in sent.items():
+            if name not in done and not name.startswith(later or ("none",)):
+                done.add(name)
+                cp.wait_send()
 
     z_start()
     own_term(4)
@@ -454,13 +473,14 @@
     kv_half(1, 1)
     share("q", 4)
     kv_half(0, 1)
+    all_sent("c", "d0", "e", "h", "gpo4", "gmq4")
     finish_low()
     kv_finish()
-    finish_high()
+    finish_high("a")
+    finish_high("b")
     arrived("gpo4", "gmq4")
 
-    for cp in sent.values():
-        cp.wait_send()
+    all_sent()
 
 
 def write_out(kv, grad, params, moment, weights, kv_out, grad_out, np_out, nm_out, lw_out, sem):
@@ -512,7 +532,7 @@
         pltpu.SemaphoreType.DMA((len(MESSAGES),)),
         pltpu.SemaphoreType.DMA((len(MESSAGES),)),
         pltpu.SemaphoreType.DMA((32,)),
-        pltpu.SemaphoreType.REGULAR((3,)),
+        pltpu.SemaphoreType.REGULAR((7,)),
     ]
     operands = (inputs, projection, cotangent, pseudo_grad, outer_params, outer_momentum)
     operands = [pltpu.with_memory_space_constraint(a, pltpu.HBM) for a in operands]

time: 66.3 us -> 64.8 us (0.977)
  Pallas kernels: 65.6 us -> 63.9 us
    pallas_call x1, Pallas kernels: 63.7 us -> 62.1 us  [on_device(): pl.pallas_call(kernel, out_shape=(vm((TOK, KV), bf16), vm((ROWS, KV), f32...]
where the time goes in v4:
time: 64.8 us; the launch traced here: 64.6 us
  Pallas kernels  63.9 us (99%)
    pallas_call x1, Pallas kernels, on_device(): pl.pallas_call(kernel, out_shape=(vm((TOK, KV), bf16), vm((ROWS, KV), f32...  62.1 us
    pallas_call x1, Pallas kernels, on_device(): pl.pallas_call(write_out, out_shape=(jax.ShapeDtypeStruct((TOK, KV), bf16...  1.82 us

profile of v4, /device:TPU:24, one launch (start us, length us, event | category | flops | bytes accessed | tf_op | source)
XLA Modules:
  0.0 64.6 jit_solution(7056060592745137918)
XLA Ops:
  0.6 62.1 %shard_map.101 = (bf16[384,1024]{1,0:T(8,128)(2,1)S(1)}, f32[256,1024]{1,0:T(8,128)S(1)}, f32[128,256]{1,0:T(8,128)S(1)}, f32[128,256]{1,0:T(8,128)S(1)}, bf16[8,2,128,256]{3,2,1,0:T(8,128)(2,1)S(1)}) custom-call(bf16[384,4096]{1,0:T(8,128)(2,1)} %x_hbm.1, bf16[1,256,1024]{2,1,0:T(8,128)(2,1)} %w_hbm.1, bf16[384,1024]{1,0:T(8,128)(2,1)} %c_hbm.1, ...), custom_call_target="tpu_custom_call" | custom-call | flops 6000000000 | bytes 30000000 | tf_op jit(solution)/shard_map/pallas_call | solution.py:539
  62.7 1.8 %shard_map.102 = (bf16[384,1024]{1,0:T(8,128)(2,1)}, f32[1,256,1024]{2,1,0:T(8,128)}, f32[128,256]{1,0:T(8,128)}, f32[128,256]{1,0:T(8,128)}, bf16[128,4096]{1,0:T(8,128)(2,1)}) custom-call(bf16[384,1024]{1,0:T(8,128)(2,1)S(1)} %get-tuple-element.10.kv, f32[256,1024]{1,0:T(8,128)S(1)} %get-tuple-element.11.grad, f32[128,256]{1,0:T(8,128)S(1)} %get-tuple-element.12.params, ...), custom_call_target="tpu_custom_call" | custom-call | tf_op jit(solution)/shard_map/pallas_call | solution.py:557

commit v5 on v4

--- a/solution.py
+++ b/solution.py
@@ -74,7 +74,7 @@
     barrier = pltpu.get_barrier_semaphore()
     NEAR = ("xp", "xm", "y", "yl", "zp", "zm", "sib")
     device_of = dict(xp=XP, xm=XM, y=Y, yl=YL, zp=ZP, zm=ZM, sib=SIB)
-    first = dict(xp=x < 3, xm=x == 0, y=yh == 0, yl=ylo == 0, zp=z < 7, zm=z == 0, sib=c == 1)
+    first = dict(xp=x < 3, xm=x == 0, y=yh == 0, yl=ylo == 0, zp=z < 7, zm=z == 0, sib=c == 0)
     back = dict(xp="xm", xm="xp", y="y", yl="yl", zp="zm", zm="zp", sib="sib")
 
     for k in NEAR:

time: 64.8 us -> 64.8 us (level)
  no operation moved by 1% of the time
where the time goes in v5:
time: 64.8 us; the launch traced here: 64.6 us
  Pallas kernels  63.9 us (99%)
    pallas_call x1, Pallas kernels, on_device(): pl.pallas_call(kernel, out_shape=(vm((TOK, KV), bf16), vm((ROWS, KV), f32...  62.1 us
    pallas_call x1, Pallas kernels, on_device(): pl.pallas_call(write_out, out_shape=(jax.ShapeDtypeStruct((TOK, KV), bf16...  1.82 us

profile of v5, /device:TPU:24, one launch (start us, length us, event | category | flops | bytes accessed | tf_op | source)
XLA Modules:
  0.0 64.6 jit_solution(116632156601387165)
XLA Ops:
  0.6 62.1 %shard_map.101 = (bf16[384,1024]{1,0:T(8,128)(2,1)S(1)}, f32[256,1024]{1,0:T(8,128)S(1)}, f32[128,256]{1,0:T(8,128)S(1)}, f32[128,256]{1,0:T(8,128)S(1)}, bf16[8,2,128,256]{3,2,1,0:T(8,128)(2,1)S(1)}) custom-call(bf16[384,4096]{1,0:T(8,128)(2,1)} %x_hbm.1, bf16[1,256,1024]{2,1,0:T(8,128)(2,1)} %w_hbm.1, bf16[384,1024]{1,0:T(8,128)(2,1)} %c_hbm.1, ...), custom_call_target="tpu_custom_call" | custom-call | flops 6000000000 | bytes 30000000 | tf_op jit(solution)/shard_map/pallas_call | solution.py:539
  62.7 1.8 %shard_map.102 = (bf16[384,1024]{1,0:T(8,128)(2,1)}, f32[1,256,1024]{2,1,0:T(8,128)}, f32[128,256]{1,0:T(8,128)}, f32[128,256]{1,0:T(8,128)}, bf16[128,4096]{1,0:T(8,128)(2,1)}) custom-call(bf16[384,1024]{1,0:T(8,128)(2,1)S(1)} %get-tuple-element.10.kv, f32[256,1024]{1,0:T(8,128)S(1)} %get-tuple-element.11.grad, f32[128,256]{1,0:T(8,128)S(1)} %get-tuple-element.12.params, ...), custom_call_target="tpu_custom_call" | custom-call | tf_op jit(solution)/shard_map/pallas_call | solution.py:557
